TPU v7x, 256 devices: a whole 4x4x8 slice. The times are simulated.
256 devices in a mesh: dp: 32 (over y, z), expert: 8 (over x, core).
Axes of the slice: x: 4, y: 4, z: 8, core: 2. Of those that a mesh axis runs over, the one named last changes fastest.
Arguments:
- residual: bfloat16 [32768, 3072], P(('dp', 'expert')), may hold values from -36 to 36
- context: bfloat16 [32768, 24, 128], P('dp', 'expert'), may hold values from -6 to 6
- master: float32 [24, 128, 3072], P('expert', 'dp'), may hold values from -0.109375 to 0.109375
- grad: float32 [24, 128, 3072], P('expert', 'dp'), may hold values from -6 to 6
- moment: float32 [24, 128, 3072], P('expert', 'dp'), may hold values from -1.8 to 1.8
- second: float32 [24, 128, 3072], P('expert', 'dp'), may hold values from 0.0005 to 0.02
- gain: float32 [3072], replicated, may hold values from 0.5 to 1.5
- token_ids: int32 [32768], P(('dp', 'expert')), may hold values from 0 to 51199
- table_one: int32 [51200], replicated, may hold values from 0 to 31
- table_two: int32 [51200], replicated, may hold values from 0 to 31
- w_in: bfloat16 [32, 1536, 5120], P('dp', None, 'expert'), may hold values from -0.15625 to 0.15625
- w_out: bfloat16 [32, 5120, 1536], P('dp', 'expert'), may hold values from -0.078125 to 0.078125
Outputs:
- mixed: bfloat16 [32768, 3072], P(('dp', 'expert'))
All inputs are finite; a program needn't handle non-finite values.
Results may differ from a plain program's by a relative error of at most 0.009.
Values may be sent and summed in bfloat16 or wider, within the bound.
No kernel may reach another device: no remote copies, remote signals or barrier semaphores. Data moves between devices by JAX's collectives and lax.ppermute only.
A program may use at most 64 MiB of HBM per device.

v0:
```python
import jax
import jax.numpy as jnp
from jax import lax
from jax.sharding import PartitionSpec as P

lr_rate = 0.01
beta_one = 0.9
beta_two = 0.999
adam_step = 10.0
eps_adam = 1e-08
eps_norm = 1e-05


def adam_weight(master, grad, moment, second):
    new_moment = beta_one * moment + (1.0 - beta_one) * grad
    new_second = beta_two * second + (1.0 - beta_two) * grad * grad
    corr_one = 1.0 - beta_one**adam_step
    corr_two = 1.0 - beta_two**adam_step
    update = new_moment / corr_one / (jnp.sqrt(new_second / corr_two) + eps_adam)
    return (master - lr_rate * update).astype(jnp.bfloat16)


def slot_tables(routes_of, experts, capacity):
    onehot = (routes_of[..., None] == jnp.arange(experts, dtype=jnp.int32)).astype(jnp.int32)
    before = jnp.cumsum(onehot, axis=-2) - onehot
    slot_rank = jnp.sum(before * onehot, axis=-1)
    match_expert = routes_of[..., None, :] == jnp.arange(experts, dtype=jnp.int32)[:, None]
    match_slot = slot_rank[..., None, :] == jnp.arange(capacity, dtype=jnp.int32)[:, None]
    return (match_expert[..., :, None, :] & match_slot[..., None, :, :]).astype(jnp.bfloat16)


def on_device(
    residual,
    context,
    master,
    grad,
    moment,
    second,
    gain,
    token_ids,
    table_one,
    table_two,
    w_in,
    w_out,
):
    experts = lax.axis_size("dp") * w_in.shape[0]
    tok_count = residual.shape[0]
    model_width = residual.shape[1]
    half_width = model_width // 2
    capacity = max(2, 5 * tok_count // (4 * experts))
    fresh = adam_weight(master, grad, moment, second)
    weight_all = lax.all_gather(fresh, "dp", axis=1, tiled=True)
    weight_rows = weight_all.reshape(-1, model_width)
    ctx_rows = context.reshape(context.shape[0], -1)
    attn = lax.psum_scatter(
        jnp.dot(ctx_rows, weight_rows, preferred_element_type=jnp.float32).astype(jnp.bfloat16),
        "expert",
        scatter_dimension=0,
        tiled=True,
    ).astype(jnp.float32)
    state = residual.astype(jnp.float32) + attn
    scale = lax.rsqrt(jnp.mean(state * state, axis=-1, keepdims=True) + eps_norm)
    normed = (state * scale * gain).astype(jnp.bfloat16)
    halves = normed.reshape(tok_count, 2, half_width)
    routes = jnp.stack([table_one[token_ids], table_two[token_ids]])
    dispatch = slot_tables(routes, experts, capacity)
    outgoing = jnp.einsum(
        "kest,tkd->eksd", dispatch, halves, preferred_element_type=jnp.float32
    ).astype(jnp.bfloat16)
    arrived = lax.all_to_all(outgoing, "dp", split_axis=0, concat_axis=0, tiled=True)
    rows_here = arrived.reshape(-1, half_width)
    inner = jnp.dot(
        lax.all_gather(rows_here, "expert", axis=0, tiled=True),
        w_in[0],
        preferred_element_type=jnp.float32,
    )
    hidden = jax.nn.gelu(inner, approximate=True).astype(jnp.bfloat16)
    partial_rows = jnp.dot(hidden, w_out[0], preferred_element_type=jnp.float32)
    expert_out = lax.psum_scatter(
        partial_rows.astype(jnp.bfloat16), "expert", scatter_dimension=0, tiled=True
    )
    shaped = expert_out.reshape(experts, 2, capacity, half_width)
    returned = lax.all_to_all(shaped, "dp", split_axis=0, concat_axis=0, tiled=True)
    routed = jnp.einsum("kest,eksd->tkd", dispatch, returned, preferred_element_type=jnp.float32)
    routed = routed.reshape(tok_count, model_width)
    return (state + routed).astype(jnp.bfloat16)


def solution(mesh):
    return jax.shard_map(
        on_device,
        mesh=mesh,
        in_specs=(
            P(("dp", "expert"), None),
            P("dp", "expert", None),
            P("expert", "dp", None),
            P("expert", "dp", None),
            P("expert", "dp", None),
            P("expert", "dp", None),
            P(),
            P(("dp", "expert")),
            P(),
            P(),
            P("dp", None, "expert"),
            P("dp", "expert", None),
        ),
        out_specs=P(("dp", "expert"), None),
        check_vma=False,
    )
```

profile of v0, /device:TPU:32, one launch (start us, length us, event | category | flops | bytes accessed | tf_op | source)
XLA Modules:
  0.0 366.9 jit_solution(9188723289170814963)
XLA Ops:
  6.5 1.5 subtract_convert_fusion
  8.0 0.7 copy.49
  8.8 83.0 %all-gather.3.cloned.1.call-done = bf16[3,128,3072]{2,0,1:T(4,128)(2,1)} async-done(((bf16[3,4,3072]{2,0,1:T(4,128)(2,1)}), bf16[3,128,3072]{2,0,1:T(4,128)(2,1)}) %all-gather.3.cloned.1.call-update) | async-done | bytes 2359312 | tf_op jit(solution)/shard_map/all_gather | solution.py:52
  91.8 8.5 %fusion.8 = bf16[1024,3072]{0,1:T(8,128)(2,1)} fusion(bf16[1024,3,128]{2,0,1:T(8,128)(2,1)} %param.13, bf16[3,128,3072]{2,0,1:T(4,128)(2,1)} %all-gather.3.cloned.1.call-done), kind=kOutput, calls=%fused_computation.13 | convolution fusion | flops 2419064832 | bytes 9437184 | tf_op jit(solution)/shard_map/dot_general | solution.py:56
  100.3 8.6 %copy.61 = bf16[1024,3072]{1,0:T(8,128)(2,1)} copy(bf16[1024,3072]{0,1:T(8,128)(2,1)} %fusion.8) | data formatting | bytes 12582912
  109.0 0.6 copy-done.4
  109.8 1.1 gather_fusion.1
  111.0 1.1 gather_fusion
  113.1 38.4 %reduce-scatter.7.cloned.1.call-done = bf16[128,3072]{1,0:T(8,128)(2,1)} async-done(((bf16[1024,3072]{1,0:T(8,128)(2,1)}), bf16[128,3072]{1,0:T(8,128)(2,1)}) %reduce-scatter.7.cloned.1.call-update) | async-done | bytes 786448
  151.4 1.5 copy.62
  153.4 1.2 multiply_convert_fusion
  155.0 1.0 copy.52
  156.0 36.5 %all_to_all.10 = bf16[32,2,5,1536]{3,1,2,0:T(2,128)(2,1)S(1)} all-to-all(bf16[32,2,5,1536]{3,1,2,0:T(2,128)(2,1)S(1)} %copy.52), channel_id=1, replica_groups=mesh['dp'=32,'expert'=8] {'dp'}, dimensions={0} | all-to-all | bytes 1966080 | tf_op jit(solution)/shard_map/all_to_all | solution.py:70
  192.5 1.4 copy.53
  194.0 2.4 reshape.33
  196.6 45.8 %all-gather.5.cloned.1.call-done = bf16[2560,1536]{1,0:T(8,128)(2,1)} async-done(((bf16[320,1536]{1,0:T(8,128)(2,1)}), bf16[2560,1536]{1,0:T(8,128)(2,1)}) %all-gather.5.cloned.1.call-update) | async-done | bytes 7864336 | tf_op jit(solution)/shard_map/all_gather | solution.py:73
  242.5 19.6 %convolution_convert_fusion = bf16[2560,1536]{1,0:T(8,128)(2,1)} fusion(bf16[1,640,1536]{2,1,0:T(8,128)(2,1)S(1)} %copy-done, bf16[2560,1536]{1,0:T(8,128)(2,1)} %all-gather.5.cloned.1.call-done, bf16[1,1536,640]{2,1,0:T(8,128)(2,1)} %param.22), kind=kOutput, calls=%fused_computation.3 | convolution fusion | flops 10085007360 | bytes 19660800 | tf_op jit(solution)/shard_map/dot_general | solution.py:78
  262.1 52.8 %reduce-scatter.5.cloned.1.call-done = bf16[320,1536]{1,0:T(8,128)(2,1)} async-done(((bf16[2560,1536]{1,0:T(8,128)(2,1)}), bf16[320,1536]{1,0:T(8,128)(2,1)}) %reduce-scatter.5.cloned.1.call-update) | async-done | bytes 983056 | tf_op jit(solution)/shard_map/reduce_scatter | solution.py:79
  314.9 2.4 reshape.34
  317.3 2.2 copy.54
  319.6 36.5 %all_to_all.11 = bf16[32,2,5,1536]{3,1,2,0:T(2,128)(2,1)S(1)} all-to-all(bf16[32,2,5,1536]{3,1,2,0:T(2,128)(2,1)S(1)} %copy.54), channel_id=1, replica_groups=mesh['dp'=32,'expert'=8] {'dp'}, dimensions={0} | all-to-all | bytes 1966080 | tf_op jit(solution)/shard_map/all_to_all | solution.py:83
  356.1 0.7 fusion.24
  356.8 1.2 fusion.23
  358.1 2.3 copy.56
  (29 shorter events, 2.4 us)
Async XLA Ops:
  6.5 235.9 %copy-start = (bf16[1,640,1536]{2,1,0:T(8,128)(2,1)S(1)}, bf16[1,640,1536]{2,1,0:T(8,128)(2,1)}, u32[]{:S(2)}) copy-start(bf16[1,640,1536]{2,1,0:T(8,128)(2,1)} %param.23) | copy-start | bytes 5898244
  6.5 85.2 %all-gather.3.cloned.1.call-start = ((), (), s32[]{:S(2)}) async-start(), calls=%async_computation.4 | async-start | bytes 3244032 | tf_op jit(solution)/shard_map/all_gather | solution.py:52
  8.7 142.7 %reduce-scatter.7.cloned.1.call-start = ((), (), s32[]{:S(2)}) async-start(), calls=%async_computation.7 | async-start | bytes 7077888
  108.9 0.7 copy-start.4
  108.9 0.9 copy-start.1
  108.9 2.1 copy-start.2
  108.9 3.3 copy-start.3
  108.9 133.5 %all-gather.5.cloned.1.call-start = ((), (), s32[]{:S(2)}) async-start(), calls=%async_computation.5 | async-start | bytes 8847360 | tf_op jit(solution)/shard_map/all_gather | solution.py:73
  196.4 118.5 %reduce-scatter.5.cloned.1.call-start = ((), (), s32[]{:S(2)}) async-start(), calls=%async_computation.6 | async-start | bytes 8847360 | tf_op jit(solution)/shard_map/reduce_scatter | solution.py:79
Sparse Core Ops, SparseCore 0:
  9.9 81.7 all-gather.2
  109.0 42.3 reduce-scatter.6
  196.5 45.8 all-gather.4
  262.2 52.6 reduce-scatter.4
where the time goes:
time: 367 us
  waiting for transfers between devices  220 us (60%)
  blocking collectives  73.1 us (20%)
  matrix products  29.3 us (8%)
  local copies, waits for them, and re-layouts  26.1 us (7%)
  between operations  13.2 us (4%)
  other arithmetic  4.85 us (1%)
    all_gather x1, waiting for transfers between devices, on_device(): weight_all = lax.all_gather(fresh, 'dp', axis=1, tiled=True)  83 us
    reduce_scatter x1, waiting for transfers between devices, on_device(): lax.psum_scatter(partial_rows.astype(jnp.bfloat16), 'expert', scatter_dim...  52.8 us
    all_gather x1, waiting for transfers between devices, on_device(): lax.all_gather(rows_here, 'expert', axis=0, tiled=True)  45.8 us
    unnamed x5, waiting for transfers between devices  38.4 us
    all_to_all x1, blocking collectives, on_device(): lax.all_to_all(shaped, 'dp', split_axis=0, concat_axis=0, tiled=True)  36.5 us
    all_to_all x1, blocking collectives, on_device(): lax.all_to_all(outgoing, 'dp', split_axis=0, concat_axis=0, tiled=True)  36.5 us
    dot_general x1, matrix products, on_device(): partial_rows = jnp.dot(hidden, w_out[0], preferred_element_type=jnp.float32)  19.6 us
    unnamed x13, local copies, waits for them, and re-layouts  11.4 us
  transfers between devices with their start and end apart: 4, of which 4 were waited for; matrix products, arithmetic and copies ran while one was open for 1% of the time, Pallas kernels for 0%

commit v1 on v0

--- a/solution.py
+++ b/solution.py
@@ -21,9 +21,10 @@
 
 
 def slot_tables(routes_of, experts, capacity):
-    onehot = (routes_of[..., None] == jnp.arange(experts, dtype=jnp.int32)).astype(jnp.int32)
-    before = jnp.cumsum(onehot, axis=-2) - onehot
-    slot_rank = jnp.sum(before * onehot, axis=-1)
+    tokens = routes_of.shape[-1]
+    same = routes_of[..., :, None] == routes_of[..., None, :]
+    earlier = jnp.arange(tokens)[None, :] < jnp.arange(tokens)[:, None]
+    slot_rank = jnp.sum((same & earlier).astype(jnp.int32), axis=-1)
     match_expert = routes_of[..., None, :] == jnp.arange(experts, dtype=jnp.int32)[:, None]
     match_slot = slot_rank[..., None, :] == jnp.arange(capacity, dtype=jnp.int32)[:, None]
     return (match_expert[..., :, None, :] & match_slot[..., None, :, :]).astype(jnp.bfloat16)

time: 367 us -> 367 us (level)
  no operation moved by 1% of the time
where the time goes in v1:
time: 367 us
  waiting for transfers between devices  220 us (60%)
  blocking collectives  73.1 us (20%)
  matrix products  29.3 us (8%)
  local copies, waits for them, and re-layouts  26.1 us (7%)
  between operations  13.2 us (4%)
  other arithmetic  4.57 us (1%)
    all_gather x1, waiting for transfers between devices, on_device(): weight_all = lax.all_gather(fresh, 'dp', axis=1, tiled=True)  83 us
    reduce_scatter x1, waiting for transfers between devices, on_device(): lax.psum_scatter(partial_rows.astype(jnp.bfloat16), 'expert', scatter_dim...  52.8 us
    all_gather x1, waiting for transfers between devices, on_device(): lax.all_gather(rows_here, 'expert', axis=0, tiled=True)  45.8 us
    unnamed x5, waiting for transfers between devices  38.7 us
    all_to_all x1, blocking collectives, on_device(): lax.all_to_all(shaped, 'dp', split_axis=0, concat_axis=0, tiled=True)  36.6 us
    all_to_all x1, blocking collectives, on_device(): lax.all_to_all(outgoing, 'dp', split_axis=0, concat_axis=0, tiled=True)  36.5 us
    dot_general x1, matrix products, on_device(): partial_rows = jnp.dot(hidden, w_out[0], preferred_element_type=jnp.float32)  19.6 us
    unnamed x13, local copies, waits for them, and re-layouts  11.4 us
  transfers between devices with their start and end apart: 4, of which 4 were waited for; matrix products, arithmetic and copies ran while one was open for 1% of the time, Pallas kernels for 0%

profile of v1, /device:TPU:32, one launch (start us, length us, event | category | flops | bytes accessed | tf_op | source)
XLA Modules:
  0.0 366.9 jit_solution(7557003180578540496)
XLA Ops:
  6.5 1.5 subtract_convert_fusion
  8.0 0.7 copy.63
  8.8 83.0 %all-gather.3.cloned.1.call-done = bf16[3,128,3072]{2,0,1:T(4,128)(2,1)} async-done(((bf16[3,4,3072]{2,0,1:T(4,128)(2,1)}), bf16[3,128,3072]{2,0,1:T(4,128)(2,1)}) %all-gather.3.cloned.1.call-update) | async-done | bytes 2359312 | tf_op jit(solution)/shard_map/all_gather | solution.py:53
  91.8 8.5 %fusion.8 = bf16[1024,3072]{0,1:T(8,128)(2,1)} fusion(bf16[1024,3,128]{2,0,1:T(8,128)(2,1)} %param.13, bf16[3,128,3072]{2,0,1:T(4,128)(2,1)} %all-gather.3.cloned.1.call-done), kind=kOutput, calls=%fused_computation.13 | convolution fusion | flops 2419064832 | bytes 9437184 | tf_op jit(solution)/shard_map/dot_general | solution.py:57
  100.3 8.6 %copy.75 = bf16[1024,3072]{1,0:T(8,128)(2,1)} copy(bf16[1024,3072]{0,1:T(8,128)(2,1)} %fusion.8) | data formatting | bytes 12582912
  109.0 0.6 copy-done.4
  109.8 1.1 gather_fusion.1
  111.0 1.1 gather_fusion
  112.8 38.7 %reduce-scatter.7.cloned.1.call-done = bf16[128,3072]{1,0:T(8,128)(2,1)} async-done(((bf16[1024,3072]{1,0:T(8,128)(2,1)}), bf16[128,3072]{1,0:T(8,128)(2,1)}) %reduce-scatter.7.cloned.1.call-update) | async-done | bytes 786448
  151.5 1.5 copy.76
  153.4 1.2 multiply_convert_fusion
  155.0 1.0 copy.66
  156.0 36.5 %all_to_all.10 = bf16[32,2,5,1536]{3,1,2,0:T(2,128)(2,1)S(1)} all-to-all(bf16[32,2,5,1536]{3,1,2,0:T(2,128)(2,1)S(1)} %copy.66), channel_id=1, replica_groups=mesh['dp'=32,'expert'=8] {'dp'}, dimensions={0} | all-to-all | bytes 1966080 | tf_op jit(solution)/shard_map/all_to_all | solution.py:71
  192.6 1.4 copy.67
  194.0 2.4 reshape.45
  196.6 45.8 %all-gather.5.cloned.1.call-done = bf16[2560,1536]{1,0:T(8,128)(2,1)} async-done(((bf16[320,1536]{1,0:T(8,128)(2,1)}), bf16[2560,1536]{1,0:T(8,128)(2,1)}) %all-gather.5.cloned.1.call-update) | async-done | bytes 7864336 | tf_op jit(solution)/shard_map/all_gather | solution.py:74
  242.4 19.6 %convolution_convert_fusion = bf16[2560,1536]{1,0:T(8,128)(2,1)} fusion(bf16[1,640,1536]{2,1,0:T(8,128)(2,1)S(1)} %copy-done, bf16[2560,1536]{1,0:T(8,128)(2,1)} %all-gather.5.cloned.1.call-done, bf16[1,1536,640]{2,1,0:T(8,128)(2,1)} %param.22), kind=kOutput, calls=%fused_computation.3 | convolution fusion | flops 10085007360 | bytes 19660800 | tf_op jit(solution)/shard_map/dot_general | solution.py:79
  262.1 52.8 %reduce-scatter.5.cloned.1.call-done = bf16[320,1536]{1,0:T(8,128)(2,1)} async-done(((bf16[2560,1536]{1,0:T(8,128)(2,1)}), bf16[320,1536]{1,0:T(8,128)(2,1)}) %reduce-scatter.5.cloned.1.call-update) | async-done | bytes 983056 | tf_op jit(solution)/shard_map/reduce_scatter | solution.py:80
  314.9 2.4 reshape.46
  317.3 2.2 copy.68
  319.5 36.6 %all_to_all.11 = bf16[32,2,5,1536]{3,1,2,0:T(2,128)(2,1)S(1)} all-to-all(bf16[32,2,5,1536]{3,1,2,0:T(2,128)(2,1)S(1)} %copy.68), channel_id=1, replica_groups=mesh['dp'=32,'expert'=8] {'dp'}, dimensions={0} | all-to-all | bytes 1966080 | tf_op jit(solution)/shard_map/all_to_all | solution.py:84
  356.1 0.7 fusion.24
  356.8 1.2 fusion.23
  358.0 2.3 copy.70
  (28 shorter events, 2.1 us)
Async XLA Ops:
  6.5 235.9 %copy-start = (bf16[1,640,1536]{2,1,0:T(8,128)(2,1)S(1)}, bf16[1,640,1536]{2,1,0:T(8,128)(2,1)}, u32[]{:S(2)}) copy-start(bf16[1,640,1536]{2,1,0:T(8,128)(2,1)} %param.23) | copy-start | bytes 5898244
  6.5 85.2 %all-gather.3.cloned.1.call-start = ((), (), s32[]{:S(2)}) async-start(), calls=%async_computation.4 | async-start | bytes 3244032 | tf_op jit(solution)/shard_map/all_gather | solution.py:53
  8.7 142.7 %reduce-scatter.7.cloned.1.call-start = ((), (), s32[]{:S(2)}) async-start(), calls=%async_computation.7 | async-start | bytes 7077888
  108.9 0.7 copy-start.4
  108.9 0.9 copy-start.1
  108.9 2.1 copy-start.2
  108.9 3.3 copy-start.3
  108.9 133.5 %all-gather.5.cloned.1.call-start = ((), (), s32[]{:S(2)}) async-start(), calls=%async_computation.5 | async-start | bytes 8847360 | tf_op jit(solution)/shard_map/all_gather | solution.py:74
  196.4 118.5 %reduce-scatter.5.cloned.1.call-start = ((), (), s32[]{:S(2)}) async-start(), calls=%async_computation.6 | async-start | bytes 8847360 | tf_op jit(solution)/shard_map/reduce_scatter | solution.py:80
Sparse Core Ops, SparseCore 0:
  9.9 81.7 all-gather.2
  109.1 42.3 reduce-scatter.6
  196.5 45.8 all-gather.4
  262.2 52.6 reduce-scatter.4
